TPU v7x, 32 devices: a whole 2x2x4 slice. The times are simulated.
32 devices in a mesh: tensor: 2 (over y), expert: 16 (over z, x, core).
Axes of the slice: x: 2, y: 2, z: 4, core: 2. Of those that a mesh axis runs over, the one named last changes fastest.
Arguments:
- attn_partial: bfloat16 [2, 256, 4096], P('tensor', 'expert'), may hold values from -6 to 6
- norm_gain: float32 [4096], replicated, may hold values from 0.1 to 1.9
- expert_ids: int32 [256, 8], P('expert'), may hold values from 0 to 15, all different within a row; in each aligned block of 8 rows (0 to 7, 8 to 15, ...) at most 8 rows name the same one
- route_weights: float32 [256, 8], P('expert'), may hold values from 0.1 to 1
- gate_proj: bfloat16 [16, 4096, 1024], P('expert', None, 'tensor'), may hold values from -0.09375 to 0.09375
- up_proj: bfloat16 [16, 4096, 1024], P('expert', None, 'tensor'), may hold values from -0.09375 to 0.09375
- down_proj: bfloat16 [16, 1024, 4096], P('expert', None, 'tensor'), may hold values from -0.1875 to 0.1875
Outputs:
- combined: bfloat16 [256, 4096], P(('expert', 'tensor'))
Inputs may be any that keep to these rules, and one draw needn't show every extreme that they name: `expert_ids`: each row names 8 different experts. In each aligned block of 8 rows (the rows of one device in the output's order) no expert is named by more than 8 rows, a bound that some block reaches.
All inputs are finite; a program needn't handle non-finite values.
Results may differ from a plain program's by a relative error of at most 0.025.
Values may be sent and summed in bfloat16 or wider, within the bound.
A program may use at most 64 MiB of HBM per device.

v0:
```python
import math

import jax
import jax.numpy as jnp
from jax import lax
from jax.sharding import PartitionSpec as P

QB = 128


def normalize_quantize(summed, norm_gain, block_width):
    row_count, feature_width = summed.shape
    mean_sq = jnp.mean(summed * summed, axis=-1, keepdims=True)
    normed = summed * lax.rsqrt(mean_sq + 1e-06) * norm_gain
    blocks = normed.reshape(row_count, feature_width // block_width, block_width)
    scales = ((jnp.max(jnp.abs(blocks), axis=-1) + 1e-06) / 448.0).astype(jnp.bfloat16)
    values = (blocks / scales.astype(jnp.float32)[:, :, None]).astype(jnp.bfloat16)
    return (values.reshape(row_count, feature_width), scales)


def route_slots(grouped_ids, expert_total):
    labels = jnp.arange(expert_total, dtype=jnp.int32)
    member = jnp.sum((grouped_ids[..., None] == labels).astype(jnp.int32), axis=-2)
    earlier = jnp.cumsum(member, axis=-2) - member
    return (member, earlier)


def place_rows(values, scales, member, earlier, capacity):
    places = jnp.arange(capacity, dtype=jnp.int32)
    chosen = (earlier[..., None] == places) & (member[..., None] > 0)
    chosen_bf = chosen.astype(jnp.bfloat16)
    send_values = jnp.einsum(
        "brec,brd->ebcd", chosen_bf, values, preferred_element_type=jnp.float32
    ).astype(jnp.bfloat16)
    send_scales = jnp.einsum(
        "brec,brn->ebcn", chosen_bf, scales, preferred_element_type=jnp.float32
    ).astype(jnp.bfloat16)
    return (send_values, send_scales)


def expert_front(values, scales, gate_matrix, up_matrix, block_width):
    row_count, feature_width = values.shape
    block_count = feature_width // block_width
    block_rows = math.gcd(row_count, 256)

    def front_block(inputs_pair):
        part_values, part_scales = inputs_pair
        pieces = part_values.reshape(block_rows, block_count, block_width).astype(jnp.float32)
        restored = (pieces * part_scales.astype(jnp.float32)[:, :, None]).astype(jnp.bfloat16)
        restored = restored.reshape(block_rows, feature_width)
        gate_act = jnp.dot(restored, gate_matrix, preferred_element_type=jnp.float32)
        up_act = jnp.dot(restored, up_matrix, preferred_element_type=jnp.float32)
        return (jax.nn.silu(gate_act) * up_act).astype(jnp.bfloat16)

    stacked = (
        values.reshape(row_count // block_rows, block_rows, feature_width),
        scales.reshape(row_count // block_rows, block_rows, block_count),
    )
    hidden = lax.map(front_block, stacked)
    return hidden.reshape(row_count, -1)


def on_device(attn_partial, norm_gain, expert_ids, route_weights, gate_proj, up_proj, down_proj):
    tensor_count = lax.axis_size("tensor")
    expert_count = lax.axis_size("expert")
    tensor_index = lax.axis_index("tensor")
    group_tokens = expert_ids.shape[0]
    top_count = expert_ids.shape[1]
    row_count = group_tokens // tensor_count
    feature_width = attn_partial.shape[2]
    block_count = feature_width // QB
    capacity = max(2, (2 * row_count * top_count + expert_count - 1) // expert_count)
    gate_matrix = gate_proj[0]
    up_matrix = up_proj[0]
    down_matrix = down_proj[0]
    hidden_share = gate_matrix.shape[1]
    column_share = down_matrix.shape[1]
    own_start = tensor_index * row_count
    own_ids = lax.dynamic_slice_in_dim(expert_ids, own_start, row_count, 0)
    own_weights = lax.dynamic_slice_in_dim(route_weights, own_start, row_count, 0)
    partial_sum = attn_partial[0].astype(jnp.float32)
    summed = lax.psum(partial_sum.astype(jnp.bfloat16), "tensor").astype(jnp.float32)
    values, scales = normalize_quantize(summed, norm_gain, QB)
    group_ids = expert_ids.reshape(tensor_count, row_count, top_count)
    member, earlier = route_slots(group_ids, expert_count)
    send_values, send_scales = place_rows(
        values.reshape(tensor_count, row_count, feature_width),
        scales.reshape(tensor_count, row_count, block_count),
        member,
        earlier,
        capacity,
    )
    recv_values, recv_scales = (
        lax.all_to_all(send_values, "expert", split_axis=0, concat_axis=0, tiled=True),
        lax.all_to_all(send_scales, "expert", split_axis=0, concat_axis=0, tiled=True),
    )
    hidden = expert_front(
        recv_values.reshape(-1, feature_width),
        recv_scales.reshape(-1, block_count),
        gate_matrix,
        up_matrix,
        QB,
    )
    hidden = hidden.reshape(expert_count, tensor_count, capacity, hidden_share)
    own_member = lax.dynamic_index_in_dim(member, tensor_index, 0, keepdims=False)
    own_earlier = lax.dynamic_index_in_dim(earlier, tensor_index, 0, keepdims=False)
    slot_total = expert_count * tensor_count * capacity
    expert_sum = jnp.dot(
        lax.all_gather(hidden.reshape(slot_total, hidden_share), "tensor", axis=1, tiled=True),
        down_matrix,
        preferred_element_type=jnp.float32,
    )
    expert_rows = expert_sum.astype(jnp.bfloat16).reshape(
        expert_count, tensor_count, capacity, column_share
    )
    returned = lax.all_to_all(
        lax.all_to_all(expert_rows, "tensor", split_axis=1, concat_axis=3, tiled=True),
        "expert",
        split_axis=0,
        concat_axis=0,
        tiled=True,
    )
    returned = returned.reshape(expert_count, capacity, feature_width)
    labels = jnp.arange(expert_count, dtype=jnp.int32)
    pair_weight = jnp.sum(
        jnp.where(own_ids[..., None] == labels, own_weights[..., None], 0.0), axis=1
    )
    places = jnp.arange(capacity, dtype=jnp.int32)
    mixing = jnp.where(
        (own_earlier[..., None] == places) & (own_member[..., None] > 0),
        pair_weight[..., None],
        0.0,
    )
    combined = jnp.einsum(
        "rec,ecd->rd", mixing, returned.astype(jnp.float32), precision=lax.Precision.HIGHEST
    )
    return combined.astype(jnp.bfloat16)


def solution(mesh):
    return jax.shard_map(
        on_device,
        mesh=mesh,
        in_specs=(
            P("tensor", "expert", None),
            P(),
            P("expert", None),
            P("expert", None),
            P("expert", None, "tensor"),
            P("expert", None, "tensor"),
            P("expert", None, "tensor"),
        ),
        out_specs=P(("expert", "tensor"), None),
        check_vma=False,
    )
```

profile of v0, /device:TPU:0, one launch (start us, length us, event | category | flops | bytes accessed | tf_op | source)
XLA Modules:
  0.0 170.9 jit_solution(2256131914601050094)
XLA Ops:
  6.5 0.0 copy-start
  6.5 0.0 all-reduce.2.cloned.1.call-start
  6.5 0.7 all-reduce.2.cloned.1.call-update
  7.3 0.8 copy.45
  8.0 0.1 convert_reduce_fusion
  8.2 25.6 %all-reduce.2.cloned.1.call-done = bf16[16,4096]{1,0:T(8,128)(2,1)} async-done(((bf16[16,4096]{1,0:T(8,128)(2,1)}), bf16[16,4096]{1,0:T(8,128)(2,1)}) %all-reduce.2.cloned.1.call-update) | async-done | bytes 131088 | tf_op jit(solution)/shard_map/psum | solution.py:82
  33.8 1.0 fusion.29
  34.8 1.0 fusion.34
  35.9 0.1 copy.47
  35.9 0.1 reduce_max.9
  36.1 0.2 fusion.26
  36.3 0.7 reshape.108
  37.0 5.6 %all-to-all-start.1 = ((bf16[16,2,256]{2,1,0:T(2,128)(2,1)}), bf16[16,2,256]{2,1,0:T(2,128)(2,1)S(1)}, u32[]{:S(2)}, u32[]{:S(2)}) async-start(bf16[16,2,256]{2,1,0:T(2,128)(2,1)} %reshape.108), calls=%async_computation.1 | async-start | bytes 32768 | tf_op jit(solution)/shard_map/all_to_all | solution.py:95
  42.7 0.1 div.28
  42.8 0.1 div.29
  42.9 1.7 fusion
  44.6 2.5 %copy.37 = bf16[16,2,8,4096]{3,2,1,0:T(8,128)(2,1)} copy(bf16[16,2,8,4096]{3,0,2,1:T(8,128)(2,1)S(1)} %fusion) | data formatting | bytes 4194304 | tf_op jit(solution)/shard_map/convert_element_type | solution.py:34
  47.1 2.1 %all-to-all-done.1 = bf16[16,2,256]{2,1,0:T(2,128)(2,1)S(1)} async-done(((bf16[16,2,256]{2,1,0:T(2,128)(2,1)}), bf16[16,2,256]{2,1,0:T(2,128)(2,1)S(1)}, u32[]{:S(2)}, u32[]{:S(2)}) %all-to-all-start.1) | async-done | bytes 16416 | tf_op jit(solution)/shard_map/all_to_all | solution.py:95
  49.2 3.9 %all-to-all-start = ((bf16[16,2,8,4096]{3,2,1,0:T(8,128)(2,1)}), bf16[16,2,8,4096]{3,2,1,0:T(8,128)(2,1)S(1)}, u32[]{:S(2)}, u32[]{:S(2)}) async-start(bf16[16,2,8,4096]{3,2,1,0:T(8,128)(2,1)} %copy.37), calls=%async_computation | async-start | bytes 4194304 | tf_op jit(solution)/shard_map/all_to_all | solution.py:94
  53.1 0.1 reshape.109
  53.2 41.0 %all-to-all-done = bf16[16,2,8,4096]{3,2,1,0:T(8,128)(2,1)S(1)} async-done(((bf16[16,2,8,4096]{3,2,1,0:T(8,128)(2,1)}), bf16[16,2,8,4096]{3,2,1,0:T(8,128)(2,1)S(1)}, u32[]{:S(2)}, u32[]{:S(2)}) %all-to-all-start) | async-done | bytes 2097184 | tf_op jit(solution)/shard_map/all_to_all | solution.py:94
  94.2 0.6 copy.48
  94.8 0.0 copy-start.2
  94.8 1.8 %fusion.2 = bf16[256,32,128]{2,1,0:T(8,128)(2,1)S(1)} fusion(f32[32,8,32,128]{3,2,1,0:T(8,128)S(1)} %copy.48, f32[256,32]{1,0:T(8,128)S(1)} %bitcast_convert_fusion), kind=kLoop, calls=%fused_computation.5 | loop fusion | flops 2097152 | bytes 6324224 | tf_op jit(solution)/shard_map/while/body/eval_jaxpr/convert_element_type | solution.py:49
  96.6 0.0 copy-start.3
  96.6 0.4 copy-done.2
  97.0 1.3 fusion.7
  98.3 0.6 copy-done.3
  98.9 0.0 copy-start.4
  98.9 1.3 fusion.21
  100.2 9.7 %all_gather.3 = bf16[256,1024]{1,0:T(8,128)(2,1)S(1)} all-gather(bf16[256,512]{1,0:T(8,128)(2,1)S(1)} %fusion.21), channel_id=1, replica_groups=mesh['tensor'=2,'expert'=16] {'tensor'}, dimensions={1}, use_global_device_ids=true | all-gather | bytes 786432 | tf_op jit(solution)/shard_map/all_gather | solution.py:109
  109.9 0.0 copy-done.4
  109.9 1.3 fusion.9
  111.2 0.0 copy-start.1
  111.2 0.1 copy.39
  111.3 16.4 %all_to_all.33 = bf16[16,2,8,2048]{3,2,0,1:T(8,128)(2,1)S(1)} all-to-all(bf16[16,2,8,2048]{3,2,0,1:T(8,128)(2,1)S(1)} %copy.39), channel_id=1, replica_groups=mesh['tensor'=2,'expert'=16] {'tensor'}, dimensions={1} | all-to-all | bytes 2097152 | tf_op jit(solution)/shard_map/all_to_all | solution.py:117
  127.7 1.1 copy.46
  128.7 10.3 %all-to-all-start.3 = ((bf16[16,1,8,4096]{3,2,1,0:T(8,128)(2,1)}), bf16[16,1,8,4096]{3,2,1,0:T(8,128)(2,1)S(1)}, u32[]{:S(2)}, u32[]{:S(2)}) async-start(bf16[16,1,8,4096]{3,2,1,0:T(8,128)(2,1)} %bitcast.19), calls=%async_computation.3 | async-start | bytes 2097152 | tf_op jit(solution)/shard_map/all_to_all | solution.py:116
  139.1 0.0 copy-done
  139.1 0.1 constant_dynamic-slice_fusion
  139.2 0.1 copy.36
  139.2 0.0 copy-done.1
  139.2 0.1 constant_dynamic-slice_fusion.1
  139.3 0.1 copy.35
  139.4 0.1 select_reduce_fusion
  139.5 22.5 %all-to-all-done.3 = bf16[16,1,8,4096]{3,2,1,0:T(8,128)(2,1)S(1)} async-done(((bf16[16,1,8,4096]{3,2,1,0:T(8,128)(2,1)}), bf16[16,1,8,4096]{3,2,1,0:T(8,128)(2,1)S(1)}, u32[]{:S(2)}, u32[]{:S(2)}) %all-to-all-start.3) | async-done | bytes 1048608 | tf_op jit(solution)/shard_map/all_to_all | solution.py:116
  162.0 2.0 %fusion.1 = bf16[8,4096]{1,0:T(8,128)(2,1)} fusion(bf16[16,1,8,4096]{3,2,1,0:T(8,128)(2,1)S(1)} %all-to-all-done.3, f32[8,16]{1,0:T(8,128)S(1)} %select_reduce_fusion, s32[8,16]{1,0:T(8,128)S(1)} %dynamic-slice_bitcast_fusion, pred[8,16]{1,0:T(8,128)(4,1)S(1)} %fusion.54), kind=kOutput, calls=%fused_computation.3 | convolution fusion | flops 50367488 | bytes 1115264 | tf_op jit(solution)/shard_map/rec,ecd->rd/dot_general | solution.py:134
  (9 shorter events, 0.1 us)
Async XLA Ops:
  6.5 132.5 %copy-start = (f32[16,8]{0,1:T(8,128)S(1)}, f32[16,8]{0,1:T(8,128)}, u32[]{:S(2)}) copy-start(f32[16,8]{0,1:T(8,128)} %param.10) | copy-start | bytes 1540
  6.5 27.2 %all-reduce.2.cloned.1.call-start = ((), (), s32[]{:S(2)}) async-start(), calls=%async_computation.4 | async-start | bytes 262144 | tf_op jit(solution)/shard_map/psum | solution.py:82
  37.0 12.1 %all-to-all-start.1 = ((bf16[16,2,256]{2,1,0:T(2,128)(2,1)}), bf16[16,2,256]{2,1,0:T(2,128)(2,1)S(1)}, u32[]{:S(2)}, u32[]{:S(2)}) async-start(bf16[16,2,256]{2,1,0:T(2,128)(2,1)} %reshape.108), calls=%async_computation.1 | async-start | bytes 32768 | tf_op jit(solution)/shard_map/all_to_all | solution.py:95
  49.2 45.0 %all-to-all-start = ((bf16[16,2,8,4096]{3,2,1,0:T(8,128)(2,1)}), bf16[16,2,8,4096]{3,2,1,0:T(8,128)(2,1)S(1)}, u32[]{:S(2)}, u32[]{:S(2)}) async-start(bf16[16,2,8,4096]{3,2,1,0:T(8,128)(2,1)} %copy.37), calls=%async_computation | async-start | bytes 4194304 | tf_op jit(solution)/shard_map/all_to_all | solution.py:94
  94.8 2.2 %copy-start.2 = (bf16[1,4096,512]{2,1,0:T(8,128)(2,1)S(1)}, bf16[1,4096,512]{2,1,0:T(8,128)(2,1)}, u32[]{:S(2)}) copy-start(bf16[1,4096,512]{2,1,0:T(8,128)(2,1)} %param.11) | copy-start | bytes 12582916
  96.6 2.3 %copy-start.3 = (bf16[1,4096,512]{2,1,0:T(8,128)(2,1)S(1)}, bf16[1,4096,512]{2,1,0:T(8,128)(2,1)}, u32[]{:S(2)}) copy-start(bf16[1,4096,512]{2,1,0:T(8,128)(2,1)} %param.12) | copy-start | bytes 12582916
  98.9 11.0 %copy-start.4 = (bf16[1,1024,2048]{2,1,0:T(8,128)(2,1)S(1)}, bf16[1,1024,2048]{2,1,0:T(8,128)(2,1)}, u32[]{:S(2)}) copy-start(bf16[1,1024,2048]{2,1,0:T(8,128)(2,1)} %param.13) | copy-start | bytes 12582916
  111.2 28.1 %copy-start.1 = (s32[16,8]{0,1:T(8,128)S(1)}, s32[16,8]{0,1:T(8,128)}, u32[]{:S(2)}) copy-start(s32[16,8]{0,1:T(8,128)} %param.9) | copy-start | bytes 1540
  128.7 33.3 %all-to-all-start.3 = ((bf16[16,1,8,4096]{3,2,1,0:T(8,128)(2,1)}), bf16[16,1,8,4096]{3,2,1,0:T(8,128)(2,1)S(1)}, u32[]{:S(2)}, u32[]{:S(2)}) async-start(bf16[16,1,8,4096]{3,2,1,0:T(8,128)(2,1)} %bitcast.19), calls=%async_computation.3 | async-start | bytes 2097152 | tf_op jit(solution)/shard_map/all_to_all | solution.py:116
Sparse Core Ops, SparseCore 0:
  9.6 24.1 all-reduce.1
where the time goes:
time: 173 us; the launch traced here: 171 us
  waiting for transfers between devices  91.9 us (53%)
  blocking collectives  26.1 us (15%)
  starting transfers between devices  19.8 us (11%)
  between operations  13.6 us (8%)
  matrix products  7.85 us (5%)
  local copies, waits for them, and re-layouts  7.39 us (4%)
  other arithmetic  4.23 us (2%)
    all_to_all x1, waiting for transfers between devices, on_device(): lax.all_to_all(send_values, 'expert', split_axis=0, concat_axis=0, tiled=...  41 us
    psum x1, waiting for transfers between devices, on_device(): lax.psum(partial_sum.astype(jnp.bfloat16), 'tensor').astype(jnp.float32)  25.6 us
    all_to_all x1, waiting for transfers between devices, on_device(): lax.all_to_all(lax.all_to_all(expert_rows, 'tensor', split_axis=1, concat...  22.5 us
    all_to_all x1, blocking collectives, on_device(): lax.all_to_all(expert_rows, 'tensor', split_axis=1, concat_axis=3, tiled=...  16.4 us
    all_to_all x1, starting transfers between devices, on_device(): lax.all_to_all(lax.all_to_all(expert_rows, 'tensor', split_axis=1, concat...  10.3 us
    all_gather x1, blocking collectives, on_device(): lax.all_gather(hidden.reshape(slot_total, hidden_share), 'tensor', axis=1...  9.65 us
    all_to_all x1, starting transfers between devices, on_device(): lax.all_to_all(send_scales, 'expert', split_axis=0, concat_axis=0, tiled=...  5.61 us
    all_to_all x1, starting transfers between devices, on_device(): lax.all_to_all(send_values, 'expert', split_axis=0, concat_axis=0, tiled=...  3.91 us
  transfers between devices with their start and end apart: 4, of which 4 were waited for; matrix products, arithmetic and copies ran while one was open for 3% of the time, Pallas kernels for 0%

commit v1 on v0

--- a/solution.py
+++ b/solution.py
@@ -1,8 +1,11 @@
+import functools
 import math
 
 import jax
 import jax.numpy as jnp
 from jax import lax
+from jax.experimental import pallas as pl
+from jax.experimental.pallas import tpu as pltpu
 from jax.sharding import PartitionSpec as P
 
 QB = 128
@@ -60,7 +63,7 @@
     return hidden.reshape(row_count, -1)
 
 
-def on_device(attn_partial, norm_gain, expert_ids, route_weights, gate_proj, up_proj, down_proj):
+def routed_on_device(attn_partial, norm_gain, expert_ids, route_weights, gate_proj, up_proj, down_proj):
     tensor_count = lax.axis_size("tensor")
     expert_count = lax.axis_size("expert")
     tensor_index = lax.axis_index("tensor")
@@ -137,6 +140,343 @@
     return combined.astype(jnp.bfloat16)
 
 
+LINES = 4
+MESH = pl.DeviceIdType.MESH
+TO_Y, TO_X, TO_CORE, TO_UP, TO_DOWN = range(5)
+
+
+def dense_kernel(
+    attn, gain, ids, weights, gate_hbm, up_hbm, down_hbm, out,
+    rows, other, gate, up, down, hid_own, hid_in, total, core_out, core_in,
+    x_keep, x_out, x_in, z_out, z_in, own_sum, swap_out, swap_in,
+    load_sem, attn_sem, row_send, row_recv, hid_sem, core_sem, x_sem, z_send, z_recv, swap_sem,
+):
+    t = lax.axis_index("tensor")
+    e = lax.axis_index("expert")
+    a, b, c = e // 4, lax.rem(e // 2, 2), lax.rem(e, 2)
+    group, width = attn.shape
+    half = width // 2
+    units = gate.shape[1]
+    peers = {
+        TO_Y: {"tensor": 1 - t, "expert": e},
+        TO_X: {"tensor": t, "expert": e + 2 - 4 * b},
+        TO_CORE: {"tensor": t, "expert": e + 1 - 2 * c},
+        TO_UP: {"tensor": t, "expert": e + 4},
+        TO_DOWN: {"tensor": t, "expert": e - 4},
+    }
+
+    loads = [
+        pltpu.make_async_copy(source, target, load_sem.at[i])
+        for i, (source, target) in enumerate(((gate_hbm, gate), (up_hbm, up), (down_hbm, down)))
+    ]
+    for load in loads:
+        load.start()
+
+    barrier = pltpu.get_barrier_semaphore()
+    for kind in (TO_Y, TO_X, TO_CORE):
+        pl.semaphore_signal(barrier, inc=1, device_id=peers[kind], device_id_type=MESH)
+    for step in range(1, LINES):
+        line_peer = {"tensor": t, "expert": lax.rem(e + 4 * step, 4 * LINES)}
+        pl.semaphore_signal(barrier, inc=1, device_id=line_peer, device_id_type=MESH)
+    pl.semaphore_wait(barrier, 2 + LINES)
+
+    swap = pltpu.make_async_remote_copy(
+        src_ref=attn, dst_ref=other, send_sem=attn_sem.at[0], recv_sem=attn_sem.at[1],
+        device_id=peers[TO_Y], device_id_type=MESH,
+    )
+    swap.start()
+    lane = lax.broadcasted_iota(jnp.int32, (group, QB), 1)
+    pair_weight = jnp.zeros((group, QB), jnp.float32)
+    for k in range(ids.shape[1]):
+        named = ids[:, k : k + 1]
+        hit = (named == lane) | (named + 4 * LINES == lane)
+        pair_weight += jnp.where(hit, weights[:, k : k + 1], 0.0)
+    high = pair_weight.astype(jnp.bfloat16).astype(jnp.float32)
+    split_weight = jnp.where(lane < 4 * LINES, high, pair_weight - high).astype(jnp.bfloat16)
+    rows[0, e, :, half:] = split_weight
+    rows[1, e, :, half:] = split_weight
+    swap.wait()
+    summed = attn[...].astype(jnp.float32) + other[...].astype(jnp.float32)
+    inverse = lax.rsqrt(jnp.mean(summed * summed, axis=-1, keepdims=True) + 1e-06)
+    for block in range(width // QB):
+        columns = slice(block * QB, (block + 1) * QB)
+        normed = summed[:, columns] * inverse * gain[:, columns]
+        largest = jnp.max(jnp.abs(normed), axis=-1, keepdims=True)
+        scale = ((largest + 1e-06) / 448.0).astype(jnp.bfloat16).astype(jnp.float32)
+        quantized = (normed / scale).astype(jnp.bfloat16).astype(jnp.float32)
+        place = block * QB % half
+        rows[block * QB // half, e, :, place : place + QB] = (quantized * scale).astype(jnp.bfloat16)
+
+    sent = []
+
+    def piece(kind, h, owner):
+        return pltpu.make_async_remote_copy(
+            src_ref=rows.at[h, owner], dst_ref=rows.at[h, owner],
+            send_sem=row_send.at[kind, h, owner], recv_sem=row_recv.at[h, owner],
+            device_id=peers[kind], device_id_type=MESH,
+        )
+
+    def send(kind, h, owner, when=None):
+        if when is None:
+            piece(kind, h, owner).start()
+        else:
+            pl.when(when)(lambda: piece(kind, h, owner).start())
+        sent.append((kind, h, owner, when))
+
+    def arrive(h, owner, when=None):
+        if when is None:
+            piece(TO_CORE, h, owner).wait_recv()
+        else:
+            pl.when(when)(lambda: piece(TO_CORE, h, owner).wait_recv())
+
+    def owner_at(line, x):
+        return line * 4 + x * 2 + c
+
+    def at(distance, sign):
+        line = a + sign * distance
+        valid = (line >= 0) & (line < LINES)
+        return jnp.clip(line, 0, LINES - 1), valid
+
+    for h in (t, 1 - t):
+        send(TO_UP, h, e, a < LINES - 1)
+        send(TO_DOWN, h, e, a > 0)
+        send(TO_X, h, e)
+        send(TO_CORE, h, e)
+    for distance in range(1, LINES + 1):
+        if distance < LINES:
+            for sign in (-1, 1):
+                line, valid = at(distance, sign)
+                owner = owner_at(line, b)
+                arrive(t, owner, valid)
+                if sign < 0:
+                    send(TO_UP, t, owner, valid & (a < LINES - 1))
+                else:
+                    send(TO_DOWN, t, owner, valid & (a > 0))
+                send(TO_X, t, owner, valid)
+                if distance >= 2:
+                    send(TO_Y, t, owner, valid)
+                send(TO_CORE, t, owner, valid)
+        if distance == 1:
+            owner = owner_at(a, 1 - b)
+            for h in (t, 1 - t):
+                arrive(h, owner)
+                send(TO_CORE, h, owner)
+            for sign in (-1, 1):
+                line, valid = at(1, sign)
+                owner = owner_at(line, b)
+                arrive(1 - t, owner, valid)
+                send(TO_CORE, 1 - t, owner, valid)
+        else:
+            for sign in (-1, 1):
+                line, valid = at(distance - 1, sign)
+                owner = owner_at(line, 1 - b)
+                arrive(t, owner, valid)
+                send(TO_Y, t, owner, valid)
+                send(TO_CORE, t, owner, valid)
+    for distance in range(1, LINES):
+        for sign in (-1, 1):
+            line, valid = at(distance, sign)
+            for x in (b, 1 - b) if distance >= 2 else (1 - b,):
+                owner = owner_at(line, x)
+                arrive(1 - t, owner, valid)
+                send(TO_CORE, 1 - t, owner, valid)
+    for line in range(LINES):
+        for x in range(2):
+            for h in range(2):
+                arrive(h, line * 4 + x * 2 + 1 - c)
+
+    loads[0].wait()
+    loads[1].wait()
+    near = a // 2
+    parts = (1 - near, near)
+    part_rows = hid_own.shape[1]
+    groups = part_rows // group
+
+    def hidden_copy(p):
+        return pltpu.make_async_remote_copy(
+            src_ref=hid_own.at[p], dst_ref=hid_in.at[p], send_sem=hid_sem.at[0, p],
+            recv_sem=hid_sem.at[1, p], device_id=peers[TO_Y], device_id_type=MESH,
+        )
+
+    def core_copy(p):
+        return pltpu.make_async_remote_copy(
+            src_ref=core_out.at[p], dst_ref=core_in.at[p], send_sem=core_sem.at[0, p],
+            recv_sem=core_sem.at[1, p], device_id=peers[TO_CORE], device_id_type=MESH,
+        )
+
+    def x_copy(p):
+        return pltpu.make_async_remote_copy(
+            src_ref=x_out.at[p], dst_ref=x_in.at[p], send_sem=x_sem.at[0, p],
+            recv_sem=x_sem.at[1, p], device_id=peers[TO_X], device_id_type=MESH,
+        )
+
+    def z_copy(line):
+        return pltpu.make_async_remote_copy(
+            src_ref=z_out.at[line], dst_ref=z_in.at[a], send_sem=z_send.at[line],
+            recv_sem=z_recv.at[a], device_id={"tensor": t, "expert": owner_at(line, b)},
+            device_id_type=MESH,
+        )
+
+    def z_arrival(line):
+        return pltpu.make_async_remote_copy(
+            src_ref=z_out.at[line], dst_ref=z_in.at[line], send_sem=z_send.at[line],
+            recv_sem=z_recv.at[line], device_id=peers[TO_X], device_id_type=MESH,
+        )
+
+    def front(p):
+        first = parts[p] * groups
+        left = rows[0, pl.ds(first, groups), :, :half].reshape(part_rows, half)
+        right = rows[1, pl.ds(first, groups), :, :half].reshape(part_rows, half)
+
+        def act(matrix):
+            return jnp.dot(left, matrix[:half, :], preferred_element_type=jnp.float32) + jnp.dot(
+                right, matrix[half:, :], preferred_element_type=jnp.float32
+            )
+
+        gate_act, up_act = act(gate), act(up)
+        hid_own[p] = (gate_act / (1.0 + jnp.exp(-gate_act)) * up_act).astype(jnp.bfloat16)
+        hidden_copy(p).start()
+
+    def back(p):
+        hidden_copy(p).wait_recv()
+        mine = pl.ds(pl.multiple_of(t * units, units), units)
+        theirs = pl.ds(pl.multiple_of((1 - t) * units, units), units)
+        acc = jnp.dot(hid_own[p], down[mine, :], preferred_element_type=jnp.float32)
+        acc += jnp.dot(hid_in[p], down[theirs, :], preferred_element_type=jnp.float32)
+        tails = rows[0, pl.ds(parts[p] * groups, groups), :, half:].reshape(part_rows, QB)
+        tail_lane = lax.broadcasted_iota(jnp.int32, (part_rows, QB), 1)
+        own = (tail_lane == e) | (tail_lane == e + 4 * LINES)
+        weight = jnp.sum(jnp.where(own, tails.astype(jnp.float32), 0.0), axis=-1, keepdims=True)
+        total[p] = (acc * weight).reshape(groups, group, half)
+        for g in range(groups // 2):
+            core_out[p, g] = total[p, 2 * g + 1 - c].astype(jnp.bfloat16)
+        core_copy(p).start()
+
+    def join_cores(p):
+        core_copy(p).wait_recv()
+        for line in range(2):
+            away = 2 * line + 1 - b
+            x_out[p, line] = (total[p, 2 * away + c] + core_in[p, away].astype(jnp.float32)).astype(jnp.bfloat16)
+        x_copy(p).start()
+        for line in range(2):
+            stay = 2 * line + b
+            x_keep[p, line] = total[p, 2 * stay + c] + core_in[p, stay].astype(jnp.float32)
+
+    def join_x(p):
+        x_copy(p).wait_recv()
+        for i in range(2):
+            line = parts[p] * 2 + i
+            joined = x_keep[p, i] + x_in[p, i].astype(jnp.float32)
+            if p == 0:
+                z_out[line] = joined.astype(jnp.bfloat16)
+                z_copy(line).start()
+            else:
+                @pl.when(line == a)
+                def _():
+                    own_sum[...] = joined
+
+                @pl.when(line != a)
+                def _():
+                    z_out[line] = joined.astype(jnp.bfloat16)
+                    z_copy(line).start()
+
+    front(0)
+    front(1)
+    loads[2].wait()
+    back(0)
+    join_cores(0)
+    back(1)
+    join_cores(1)
+    join_x(0)
+    join_x(1)
+    final = own_sum[...]
+    for step in range(1, LINES):
+        line = lax.rem(a + step, LINES)
+        z_arrival(line).wait_recv()
+        final += z_in[line].astype(jnp.float32)
+    top, low = final[: group // 2], final[group // 2 :]
+    kept = jnp.where(t == 0, top, low)
+    given = jnp.where(t == 0, low, top)
+    quarter = half // 2
+    swap_out[...] = jnp.concatenate([given[:, :quarter], given[:, quarter:]], axis=0).astype(jnp.bfloat16)
+    swap = pltpu.make_async_remote_copy(
+        src_ref=swap_out, dst_ref=swap_in, send_sem=swap_sem.at[0], recv_sem=swap_sem.at[1],
+        device_id=peers[TO_Y], device_id_type=MESH,
+    )
+    swap.start()
+    out[:, pl.ds(pl.multiple_of(t * half, half), half)] = kept.astype(jnp.bfloat16)
+    for kind, h, owner, when in sent:
+        if when is None:
+            piece(kind, h, owner).wait_send()
+        else:
+            pl.when(when)(functools.partial(lambda k, i, o: piece(k, i, o).wait_send(), kind, h, owner))
+    for p in range(2):
+        hidden_copy(p).wait_send()
+        core_copy(p).wait_send()
+        x_copy(p).wait_send()
+    for step in range(1, LINES):
+        z_copy(lax.rem(a + step, LINES)).wait_send()
+    swap.wait()
+    taken = swap_in[...].astype(jnp.float32)
+    taken = jnp.concatenate([taken[: group // 2], taken[group // 2 :]], axis=1)
+    out[:, pl.ds(pl.multiple_of((1 - t) * half, half), half)] = taken.astype(jnp.bfloat16)
+
+
+def dense_on_device(attn_partial, norm_gain, expert_ids, route_weights, gate_proj, up_proj, down_proj):
+    group, width = attn_partial.shape[1:]
+    experts = 4 * LINES
+    half, units = width // 2, gate_proj.shape[2]
+    part_rows = experts // 2 * group
+    bf, f32 = jnp.bfloat16, jnp.float32
+    dma = pltpu.SemaphoreType.DMA
+    vmem, hbm = pl.BlockSpec(memory_space=pltpu.VMEM), pl.BlockSpec(memory_space=pl.ANY)
+    return pl.pallas_call(
+        dense_kernel,
+        out_shape=jax.ShapeDtypeStruct((group // 2, width), bf),
+        in_specs=[vmem] * 4 + [hbm] * 3,
+        out_specs=vmem,
+        scratch_shapes=[
+            pltpu.VMEM((2, experts, group, half + QB), bf),
+            pltpu.VMEM((group, width), bf),
+            pltpu.VMEM(gate_proj.shape[1:], bf),
+            pltpu.VMEM(up_proj.shape[1:], bf),
+            pltpu.VMEM(down_proj.shape[1:], bf),
+            pltpu.VMEM((2, part_rows, units), bf),
+            pltpu.VMEM((2, part_rows, units), bf),
+            pltpu.VMEM((2, experts // 2, group, half), f32),
+            pltpu.VMEM((2, experts // 4, group, half), bf),
+            pltpu.VMEM((2, experts // 4, group, half), bf),
+            pltpu.VMEM((2, experts // 8, group, half), f32),
+            pltpu.VMEM((2, experts // 8, group, half), bf),
+            pltpu.VMEM((2, experts // 8, group, half), bf),
+            pltpu.VMEM((LINES, group, half), bf),
+            pltpu.VMEM((LINES, group, half), bf),
+            pltpu.VMEM((group, half), f32),
+            pltpu.VMEM((group, half // 2), bf),
+            pltpu.VMEM((group, half // 2), bf),
+            dma((3,)), dma((2,)), dma((5, 2, experts)), dma((2, experts)),
+            dma((2, 2)), dma((2, 2)), dma((2, 2)), dma((LINES,)), dma((LINES,)), dma((2,)),
+        ],
+        compiler_params=pltpu.CompilerParams(
+            collective_id=0, has_side_effects=True, vmem_limit_bytes=48 * 1024 * 1024
+        ),
+    )(
+        attn_partial[0], norm_gain.reshape(1, width), expert_ids, route_weights,
+        gate_proj[0], up_proj[0], down_proj[0],
+    )
+
+
+def on_device(attn_partial, norm_gain, expert_ids, route_weights, gate_proj, up_proj, down_proj):
+    pairs = lax.axis_size("tensor") == 2 and lax.axis_size("expert") == 4 * LINES
+    if pairs and expert_ids.shape[0] == 16 and gate_proj.shape[0] == 1:
+        return dense_on_device(
+            attn_partial, norm_gain, expert_ids, route_weights, gate_proj, up_proj, down_proj
+        )
+    return routed_on_device(
+        attn_partial, norm_gain, expert_ids, route_weights, gate_proj, up_proj, down_proj
+    )
+
+
 def solution(mesh):
     return jax.shard_map(
         on_device,

time: 173 us -> 54.8 us (0.32); the launches traced: 171 us -> 54.5 us
  waiting for transfers between devices: 91.9 us -> 0 us
  Pallas kernels: 0 us -> 48.6 us
  blocking collectives: 26.1 us -> 0 us
  starting transfers between devices: 19.8 us -> 0 us
  between operations: 13.6 us -> 0.01 us
  matrix products: 7.85 us -> 0 us
  other arithmetic: 4.23 us -> 0 us
    all_to_all x3 -> x0, waiting for transfers between devices: 65.6 us -> none  [the longest x1 41 us: on_device(): lax.all_to_all(send_values, 'expert', split_axis=0, concat_axis=0, tiled=...]
    pallas_call x0 -> x1, Pallas kernels: none -> 48.6 us  [dense_on_device(): pl.pallas_call(dense_kernel, out_shape=jax.ShapeDtypeStruct((group // 2,...]
    psum x1 -> x0, waiting for transfers between devices: 25.6 us -> none  [on_device(): lax.psum(partial_sum.astype(jnp.bfloat16), 'tensor').astype(jnp.float32)]
    all_to_all x3 -> x0, starting transfers between devices: 19.8 us -> none  [the longest x1 10.3 us: on_device(): lax.all_to_all(lax.all_to_all(expert_rows, 'tensor', split_axis=1, concat...]
    all_to_all x1 -> x0, blocking collectives: 16.4 us -> none  [on_device(): lax.all_to_all(expert_rows, 'tensor', split_axis=1, concat_axis=3, tiled=...]
    all_gather x1 -> x0, blocking collectives: 9.65 us -> none  [on_device(): lax.all_gather(hidden.reshape(slot_total, hidden_share), 'tensor', axis=1...]
    dot_general x6 -> x0, matrix products: 7.85 us -> none  [the longest x1 2.03 us: on_device(): jnp.einsum('rec,ecd->rd', mixing, returned.astype(jnp.float32), precision...]
    unnamed x14 -> x9, local copies, waits for them, and re-layouts: 2.48 us -> 5.95 us
  transfers between devices with their start and end apart: 4 -> 0, of which waited for: 4 -> 0; matrix products, arithmetic and copies ran while one was open for 3% -> 0% of each run, Pallas kernels for 0% -> 0%
where the time goes in v1:
time: 54.8 us; the launch traced here: 54.5 us
  Pallas kernels  48.6 us (89%)
  local copies, waits for them, and re-layouts  5.95 us (11%)
    pallas_call x1, Pallas kernels, dense_on_device(): pl.pallas_call(dense_kernel, out_shape=jax.ShapeDtypeStruct((group // 2,...  48.6 us
    unnamed x9, local copies, waits for them, and re-layouts  5.95 us

profile of v1, /device:TPU:0, one launch (start us, length us, event | category | flops | bytes accessed | tf_op | source)
XLA Modules:
  0.0 54.5 jit_solution(17387302579964160182)
XLA Ops:
  0.0 0.8 %copy.8.ids = s32[16,8]{1,0:T(8,128)S(1)} copy(s32[16,8]{0,1:T(8,128)} %param.9) | data formatting | bytes 1024 | tf_op args[2]
  0.8 0.8 %copy.9.weights = f32[16,8]{1,0:T(8,128)S(1)} copy(f32[16,8]{0,1:T(8,128)} %param.10) | data formatting | bytes 1024 | tf_op args[3]
  1.5 0.0 copy-start
  1.5 2.2 %copy-done = bf16[1,4096,512]{2,1,0:T(8,128)(2,1)S(1)} copy-done((bf16[1,4096,512]{2,1,0:T(8,128)(2,1)S(1)}, bf16[1,4096,512]{2,1,0:T(8,128)(2,1)}, u32[]{:S(2)}) %copy-start) | copy-done | bytes 4194328
  3.7 0.0 copy-start.1
  3.7 0.9 %copy-done.1 = bf16[1,16,4096]{2,1,0:T(8,128)(2,1)S(1)} copy-done((bf16[1,16,4096]{2,1,0:T(8,128)(2,1)S(1)}, bf16[1,16,4096]{2,1,0:T(8,128)(2,1)}, u32[]{:S(2)}) %copy-start.1) | copy-done | bytes 131096
  4.6 0.0 copy-start.2
  4.6 0.7 %copy-done.2 = f32[4096]{0:T(1024)S(1)} copy-done((f32[4096]{0:T(1024)S(1)}, f32[4096]{0:T(1024)}, u32[]{:S(2)}) %copy-start.2) | copy-done | bytes 16408
  5.3 48.6 %shard_map.73 = bf16[8,4096]{1,0:T(8,128)(2,1)S(1)} custom-call(bf16[16,4096]{1,0:T(8,128)(2,1)S(1)} %bitcast.6, f32[1,4096]{1,0:T(1,128)S(1)} %bitcast.7, s32[16,8]{1,0:T(8,128)S(1)} %copy.8.ids, f32[16,8]{1,0:T(8,128)S(1)} %copy.9.weights, bf16[4096,512]{1,0:T(8,128)(2,1)S(1)} %bitcast.5, bf16[4096,512]{1,0:T(8,128)(2,1)} %bitcast.8, ...), custom_call_target="tpu_custom_call" | custom-call | tf_op jit(solution)/shard_map/pallas_call | solution.py:433
  53.9 0.6 %copy.11 = bf16[8,4096]{1,0:T(8,128)(2,1)} copy(bf16[8,4096]{1,0:T(8,128)(2,1)S(1)} %shard_map.73) | data formatting | bytes 131072
Async XLA Ops:
  1.5 2.2 %copy-start = (bf16[1,4096,512]{2,1,0:T(8,128)(2,1)S(1)}, bf16[1,4096,512]{2,1,0:T(8,128)(2,1)}, u32[]{:S(2)}) copy-start(bf16[1,4096,512]{2,1,0:T(8,128)(2,1)} %param.11) | copy-start | bytes 12582916
  3.7 0.9 %copy-start.1 = (bf16[1,16,4096]{2,1,0:T(8,128)(2,1)S(1)}, bf16[1,16,4096]{2,1,0:T(8,128)(2,1)}, u32[]{:S(2)}) copy-start(bf16[1,16,4096]{2,1,0:T(8,128)(2,1)} %param.7) | copy-start | bytes 393220
  4.6 0.7 %copy-start.2 = (f32[4096]{0:T(1024)S(1)}, f32[4096]{0:T(1024)}, u32[]{:S(2)}) copy-start(f32[4096]{0:T(1024)} %param.8) | copy-start | bytes 49156

commit v2 on v1

--- a/solution.py
+++ b/solution.py
@@ -142,14 +142,14 @@
 
 LINES = 4
 MESH = pl.DeviceIdType.MESH
-TO_Y, TO_X, TO_CORE, TO_UP, TO_DOWN = range(5)
+TO_Y, TO_X, TO_CORE = range(3)
 
 
 def dense_kernel(
-    attn, gain, ids, weights, gate_hbm, up_hbm, down_hbm, out,
-    rows, other, gate, up, down, hid_own, hid_in, total, core_out, core_in,
-    x_keep, x_out, x_in, z_out, z_in, own_sum, swap_out, swap_in,
-    load_sem, attn_sem, row_send, row_recv, hid_sem, core_sem, x_sem, z_send, z_recv, swap_sem,
+    attn_hbm, gain_hbm, ids_hbm, weights_hbm, gate_hbm, up_hbm, down_hbm, out,
+    attn, gain, ids, weights, table, rows, other, gate, up, down, hid_own, hid_in, total, core_out, core_in,
+    x_out, x_in, z_out, z_in, swap_out, swap_in,
+    load_sem, attn_sem, row_send, line_send, row_recv, hid_sem, core_sem, x_sem, z_send, z_recv, swap_sem,
 ):
     t = lax.axis_index("tensor")
     e = lax.axis_index("expert")
@@ -161,13 +161,14 @@
         TO_Y: {"tensor": 1 - t, "expert": e},
         TO_X: {"tensor": t, "expert": e + 2 - 4 * b},
         TO_CORE: {"tensor": t, "expert": e + 1 - 2 * c},
-        TO_UP: {"tensor": t, "expert": e + 4},
-        TO_DOWN: {"tensor": t, "expert": e - 4},
     }
 
     loads = [
         pltpu.make_async_copy(source, target, load_sem.at[i])
-        for i, (source, target) in enumerate(((gate_hbm, gate), (up_hbm, up), (down_hbm, down)))
+        for i, (source, target) in enumerate((
+            (attn_hbm, attn), (ids_hbm, ids), (weights_hbm, weights), (gain_hbm, gain),
+            (gate_hbm, gate), (up_hbm, up), (down_hbm, down),
+        ))
     ]
     for load in loads:
         load.start()
@@ -181,18 +182,23 @@
     pl.semaphore_wait(barrier, 2 + LINES)
 
     swap = pltpu.make_async_remote_copy(
-        src_ref=attn, dst_ref=other, send_sem=attn_sem.at[0], recv_sem=attn_sem.at[1],
+        src_ref=attn_hbm, dst_ref=other, send_sem=attn_sem.at[0], recv_sem=attn_sem.at[1],
         device_id=peers[TO_Y], device_id_type=MESH,
     )
     swap.start()
-    lane = lax.broadcasted_iota(jnp.int32, (group, QB), 1)
-    pair_weight = jnp.zeros((group, QB), jnp.float32)
-    for k in range(ids.shape[1]):
-        named = ids[:, k : k + 1]
-        hit = (named == lane) | (named + 4 * LINES == lane)
-        pair_weight += jnp.where(hit, weights[:, k : k + 1], 0.0)
+    experts = 4 * LINES
+    for load in loads[:4]:
+        load.wait()
+    label = lax.broadcasted_iota(jnp.int32, (QB, group), 0)
+    pair_weight = jnp.zeros((QB, group), jnp.float32)
+    for k in range(ids.shape[0]):
+        named = ids[k : k + 1, :]
+        hit = (named == label) | (named + experts == label)
+        pair_weight += jnp.where(hit, weights[k : k + 1, :], 0.0)
     high = pair_weight.astype(jnp.bfloat16).astype(jnp.float32)
-    split_weight = jnp.where(lane < 4 * LINES, high, pair_weight - high).astype(jnp.bfloat16)
+    table[...] = jnp.zeros_like(table)
+    table[:, :group] = jnp.where(label < experts, high, pair_weight - high)
+    split_weight = table[...].T[:group].astype(jnp.bfloat16)
     rows[0, e, :, half:] = split_weight
     rows[1, e, :, half:] = split_weight
     swap.wait()
@@ -237,46 +243,53 @@
         valid = (line >= 0) & (line < LINES)
         return jnp.clip(line, 0, LINES - 1), valid
 
-    for h in (t, 1 - t):
-        send(TO_UP, h, e, a < LINES - 1)
-        send(TO_DOWN, h, e, a > 0)
-        send(TO_X, h, e)
-        send(TO_CORE, h, e)
-    for distance in range(1, LINES + 1):
+    def line_piece(h, line):
+        return pltpu.make_async_remote_copy(
+            src_ref=rows.at[h, e], dst_ref=rows.at[h, e], send_sem=line_send.at[h, line],
+            recv_sem=row_recv.at[h, e], device_id={"tensor": t, "expert": owner_at(line, b)},
+            device_id_type=MESH,
+        )
+
+    def along_line(act):
+        for h, distances in ((t, range(1, LINES)), (1 - t, (1,))):
+            for distance in distances:
+                for sign in (-1, 1):
+                    line, valid = at(distance, sign)
+                    pl.when(valid)(functools.partial(act, h, line))
+
+    send(TO_X, t, e)
+    send(TO_CORE, t, e)
+    along_line(lambda h, line: line_piece(h, line).start())
+    send(TO_X, 1 - t, e)
+    send(TO_CORE, 1 - t, e)
+    for distance in range(1, LINES + 2):
         if distance < LINES:
             for sign in (-1, 1):
                 line, valid = at(distance, sign)
                 owner = owner_at(line, b)
                 arrive(t, owner, valid)
-                if sign < 0:
-                    send(TO_UP, t, owner, valid & (a < LINES - 1))
-                else:
-                    send(TO_DOWN, t, owner, valid & (a > 0))
                 send(TO_X, t, owner, valid)
                 if distance >= 2:
                     send(TO_Y, t, owner, valid)
                 send(TO_CORE, t, owner, valid)
         if distance == 1:
             owner = owner_at(a, 1 - b)
-            for h in (t, 1 - t):
-                arrive(h, owner)
-                send(TO_CORE, h, owner)
-            for sign in (-1, 1):
-                line, valid = at(1, sign)
-                owner = owner_at(line, b)
-                arrive(1 - t, owner, valid)
-                send(TO_CORE, 1 - t, owner, valid)
-        else:
+            arrive(t, owner)
+            send(TO_CORE, t, owner)
+        elif distance <= LINES:
             for sign in (-1, 1):
                 line, valid = at(distance - 1, sign)
                 owner = owner_at(line, 1 - b)
                 arrive(t, owner, valid)
                 send(TO_Y, t, owner, valid)
                 send(TO_CORE, t, owner, valid)
+    owner = owner_at(a, 1 - b)
+    arrive(1 - t, owner)
+    send(TO_CORE, 1 - t, owner)
     for distance in range(1, LINES):
         for sign in (-1, 1):
             line, valid = at(distance, sign)
-            for x in (b, 1 - b) if distance >= 2 else (1 - b,):
+            for x in (b, 1 - b):
                 owner = owner_at(line, x)
                 arrive(1 - t, owner, valid)
                 send(TO_CORE, 1 - t, owner, valid)
@@ -285,12 +298,14 @@
             for h in range(2):
                 arrive(h, line * 4 + x * 2 + 1 - c)
 
-    loads[0].wait()
-    loads[1].wait()
+    loads[4].wait()
+    loads[5].wait()
     near = a // 2
     parts = (1 - near, near)
-    part_rows = hid_own.shape[1]
-    groups = part_rows // group
+    side = lax.rem(a, 2)
+    lines = (2 - 2 * near + side, 3 - 2 * near - side, 2 * near + 1 - side, a)
+    line_rows = hid_own.shape[1]
+    part_rows = 2 * line_rows
 
     def hidden_copy(p):
         return pltpu.make_async_remote_copy(
@@ -324,9 +339,8 @@
         )
 
     def front(p):
-        first = parts[p] * groups
-        left = rows[0, pl.ds(first, groups), :, :half].reshape(part_rows, half)
-        right = rows[1, pl.ds(first, groups), :, :half].reshape(part_rows, half)
+        left = rows[0, pl.ds(parts[p] * 8, 8), :, :half].reshape(part_rows, half)
+        right = rows[1, pl.ds(parts[p] * 8, 8), :, :half].reshape(part_rows, half)
 
         def act(matrix):
             return jnp.dot(left, matrix[:half, :], preferred_element_type=jnp.float32) + jnp.dot(
@@ -334,62 +348,57 @@
             )
 
         gate_act, up_act = act(gate), act(up)
-        hid_own[p] = (gate_act / (1.0 + jnp.exp(-gate_act)) * up_act).astype(jnp.bfloat16)
-        hidden_copy(p).start()
-
-    def back(p):
-        hidden_copy(p).wait_recv()
+        hidden = (gate_act / (1.0 + jnp.exp(-gate_act)) * up_act).astype(jnp.bfloat16)
+        first = lax.rem(lines[2 * p], 2)
+        hid_own[2 * p + first] = hidden[:line_rows]
+        hid_own[2 * p + 1 - first] = hidden[line_rows:]
+        for q in (2 * p, 2 * p + 1):
+            hidden_copy(q).start()
+
+    def back(q):
+        hidden_copy(q).wait_recv()
         mine = pl.ds(pl.multiple_of(t * units, units), units)
         theirs = pl.ds(pl.multiple_of((1 - t) * units, units), units)
-        acc = jnp.dot(hid_own[p], down[mine, :], preferred_element_type=jnp.float32)
-        acc += jnp.dot(hid_in[p], down[theirs, :], preferred_element_type=jnp.float32)
-        tails = rows[0, pl.ds(parts[p] * groups, groups), :, half:].reshape(part_rows, QB)
-        tail_lane = lax.broadcasted_iota(jnp.int32, (part_rows, QB), 1)
-        own = (tail_lane == e) | (tail_lane == e + 4 * LINES)
+        acc = jnp.dot(hid_own[q], down[mine, :], preferred_element_type=jnp.float32)
+        acc += jnp.dot(hid_in[q], down[theirs, :], preferred_element_type=jnp.float32)
+        tails = rows[0, pl.ds(lines[q] * 4, 4), :, half:].reshape(line_rows, QB)
+        tail_lane = lax.broadcasted_iota(jnp.int32, (line_rows, QB), 1)
+        own = (tail_lane == e) | (tail_lane == e + experts)
         weight = jnp.sum(jnp.where(own, tails.astype(jnp.float32), 0.0), axis=-1, keepdims=True)
-        total[p] = (acc * weight).reshape(groups, group, half)
-        for g in range(groups // 2):
-            core_out[p, g] = total[p, 2 * g + 1 - c].astype(jnp.bfloat16)
-        core_copy(p).start()
-
-    def join_cores(p):
-        core_copy(p).wait_recv()
-        for line in range(2):
-            away = 2 * line + 1 - b
-            x_out[p, line] = (total[p, 2 * away + c] + core_in[p, away].astype(jnp.float32)).astype(jnp.bfloat16)
-        x_copy(p).start()
-        for line in range(2):
-            stay = 2 * line + b
-            x_keep[p, line] = total[p, 2 * stay + c] + core_in[p, stay].astype(jnp.float32)
-
-    def join_x(p):
-        x_copy(p).wait_recv()
-        for i in range(2):
-            line = parts[p] * 2 + i
-            joined = x_keep[p, i] + x_in[p, i].astype(jnp.float32)
-            if p == 0:
-                z_out[line] = joined.astype(jnp.bfloat16)
-                z_copy(line).start()
-            else:
-                @pl.when(line == a)
-                def _():
-                    own_sum[...] = joined
-
-                @pl.when(line != a)
-                def _():
-                    z_out[line] = joined.astype(jnp.bfloat16)
-                    z_copy(line).start()
+        total[q] = (acc * weight).reshape(4, group, half)
+        for x in range(2):
+            core_out[q, x] = total[q, 2 * x + 1 - c].astype(jnp.bfloat16)
+        core_copy(q).start()
+
+    def join_cores(q):
+        core_copy(q).wait_recv()
+        away = 1 - b
+        x_out[q] = (total[q, 2 * away + c] + core_in[q, away].astype(jnp.float32)).astype(jnp.bfloat16)
+        x_copy(q).start()
+
+    def join_x(q):
+        x_copy(q).wait_recv()
+        joined = total[q, 2 * b + c] + core_in[q, b].astype(jnp.float32) + x_in[q].astype(jnp.float32)
+        if q == LINES - 1:
+            return joined
+        z_out[lines[q]] = joined.astype(jnp.bfloat16)
+        z_copy(lines[q]).start()
 
     front(0)
     front(1)
-    loads[2].wait()
+    loads[6].wait()
     back(0)
+    back(1)
     join_cores(0)
-    back(1)
+    back(2)
     join_cores(1)
     join_x(0)
+    back(3)
+    join_cores(2)
     join_x(1)
-    final = own_sum[...]
+    join_cores(3)
+    join_x(2)
+    final = join_x(3)
     for step in range(1, LINES):
         line = lax.rem(a + step, LINES)
         z_arrival(line).wait_recv()
@@ -410,7 +419,8 @@
             piece(kind, h, owner).wait_send()
         else:
             pl.when(when)(functools.partial(lambda k, i, o: piece(k, i, o).wait_send(), kind, h, owner))
-    for p in range(2):
+    along_line(lambda h, line: line_piece(h, line).wait_send())
+    for p in range(LINES):
         hidden_copy(p).wait_send()
         core_copy(p).wait_send()
         x_copy(p).wait_send()
@@ -426,42 +436,45 @@
     group, width = attn_partial.shape[1:]
     experts = 4 * LINES
     half, units = width // 2, gate_proj.shape[2]
-    part_rows = experts // 2 * group
+    line_rows = 4 * group
     bf, f32 = jnp.bfloat16, jnp.float32
     dma = pltpu.SemaphoreType.DMA
-    vmem, hbm = pl.BlockSpec(memory_space=pltpu.VMEM), pl.BlockSpec(memory_space=pl.ANY)
+    vmem, hbm = pl.BlockSpec(memory_space=pltpu.VMEM), pl.BlockSpec(memory_space=pltpu.HBM)
     return pl.pallas_call(
         dense_kernel,
         out_shape=jax.ShapeDtypeStruct((group // 2, width), bf),
-        in_specs=[vmem] * 4 + [hbm] * 3,
+        in_specs=[hbm] * 7,
         out_specs=vmem,
         scratch_shapes=[
+            pltpu.VMEM((group, width), bf),
+            pltpu.VMEM((1, width), f32),
+            pltpu.VMEM((expert_ids.shape[1], group), jnp.int32),
+            pltpu.VMEM((expert_ids.shape[1], group), f32),
+            pltpu.VMEM((QB, QB), f32),
             pltpu.VMEM((2, experts, group, half + QB), bf),
             pltpu.VMEM((group, width), bf),
             pltpu.VMEM(gate_proj.shape[1:], bf),
             pltpu.VMEM(up_proj.shape[1:], bf),
             pltpu.VMEM(down_proj.shape[1:], bf),
-            pltpu.VMEM((2, part_rows, units), bf),
-            pltpu.VMEM((2, part_rows, units), bf),
-            pltpu.VMEM((2, experts // 2, group, half), f32),
-            pltpu.VMEM((2, experts // 4, group, half), bf),
-            pltpu.VMEM((2, experts // 4, group, half), bf),
-            pltpu.VMEM((2, experts // 8, group, half), f32),
-            pltpu.VMEM((2, experts // 8, group, half), bf),
-            pltpu.VMEM((2, experts // 8, group, half), bf),
+            pltpu.VMEM((LINES, line_rows, units), bf),
+            pltpu.VMEM((LINES, line_rows, units), bf),
+            pltpu.VMEM((LINES, 4, group, half), f32),
+            pltpu.VMEM((LINES, 2, group, half), bf),
+            pltpu.VMEM((LINES, 2, group, half), bf),
             pltpu.VMEM((LINES, group, half), bf),
             pltpu.VMEM((LINES, group, half), bf),
-            pltpu.VMEM((group, half), f32),
+            pltpu.VMEM((LINES, group, half), bf),
+            pltpu.VMEM((LINES, group, half), bf),
             pltpu.VMEM((group, half // 2), bf),
             pltpu.VMEM((group, half // 2), bf),
-            dma((3,)), dma((2,)), dma((5, 2, experts)), dma((2, experts)),
-            dma((2, 2)), dma((2, 2)), dma((2, 2)), dma((LINES,)), dma((LINES,)), dma((2,)),
+            dma((7,)), dma((2,)), dma((3, 2, experts)), dma((2, LINES)), dma((2, experts)),
+            dma((2, LINES)), dma((2, LINES)), dma((2, LINES)), dma((LINES,)), dma((LINES,)), dma((2,)),
         ],
         compiler_params=pltpu.CompilerParams(
-            collective_id=0, has_side_effects=True, vmem_limit_bytes=48 * 1024 * 1024
+            collective_id=0, has_side_effects=True, vmem_limit_bytes=63 * 1024 * 1024
         ),
     )(
-        attn_partial[0], norm_gain.reshape(1, width), expert_ids, route_weights,
+        attn_partial[0], norm_gain.reshape(1, width), expert_ids.T, route_weights.T,
         gate_proj[0], up_proj[0], down_proj[0],
     )
 

time: 54.8 us -> 49.3 us (0.90)
  local copies, waits for them, and re-layouts: 5.95 us -> 1.47 us
  Pallas kernels: 48.6 us -> 47.6 us
    unnamed x9 -> x1, local copies, waits for them, and re-layouts: 5.95 us -> 1.47 us
    pallas_call x1, Pallas kernels: 48.6 us -> 47.6 us  [dense_on_device(): pl.pallas_call(dense_kernel, out_shape=jax.ShapeDtypeStruct((group // 2,...]
where the time goes in v2:
time: 49.3 us; the launch traced here: 49.1 us
  Pallas kernels  47.6 us (97%)
  local copies, waits for them, and re-layouts  1.47 us (3%)
    pallas_call x1, Pallas kernels, dense_on_device(): pl.pallas_call(dense_kernel, out_shape=jax.ShapeDtypeStruct((group // 2,...  47.6 us
    unnamed x1, local copies, waits for them, and re-layouts  1.47 us

profile of v2, /device:TPU:0, one launch (start us, length us, event | category | flops | bytes accessed | tf_op | source)
XLA Modules:
  0.0 49.1 jit_solution(8266036454016452831)
XLA Ops:
  0.0 47.6 %shard_map.73 = bf16[8,4096]{1,0:T(8,128)(2,1)} custom-call(bf16[16,4096]{1,0:T(8,128)(2,1)} %bitcast.10, f32[1,4096]{1,0:T(1,128)} %bitcast.11, s32[8,16]{1,0:T(8,128)} %bitcast.12, f32[8,16]{1,0:T(8,128)} %bitcast.13, bf16[4096,512]{1,0:T(8,128)(2,1)} %bitcast.7, bf16[4096,512]{1,0:T(8,128)(2,1)} %bitcast.8, bf16[1024,2048]{1,0:T(8,128)(2,1)} %bitcast.9), custom_call_target="tpu_custom_call" | custom-call | tf_op jit(solution)/shard_map/pallas_call | solution.py:443
  47.7 1.5 %copy.9 = bf16[8,4096]{1,0:T(8,128)(2,1)} copy(bf16[8,4096]{1,0:T(8,128)(2,1)} %shard_map.73) | data formatting | bytes 131072

commit v3 on v2

--- a/solution.py
+++ b/solution.py
@@ -147,7 +147,7 @@
 
 def dense_kernel(
     attn_hbm, gain_hbm, ids_hbm, weights_hbm, gate_hbm, up_hbm, down_hbm, out,
-    attn, gain, ids, weights, table, rows, other, gate, up, down, hid_own, hid_in, total, core_out, core_in,
+    attn, gain, ids, weights, table, rows, other, gate, up, down, gate_acc, up_acc, hid_own, hid_in, total, core_out, core_in,
     x_out, x_in, z_out, z_in, swap_out, swap_in,
     load_sem, attn_sem, row_send, line_send, row_recv, hid_sem, core_sem, x_sem, z_send, z_recv, swap_sem,
 ):
@@ -259,6 +259,7 @@
 
     send(TO_X, t, e)
     send(TO_CORE, t, e)
+    pair = a + 1 - 2 * lax.rem(a, 2)
     along_line(lambda h, line: line_piece(h, line).start())
     send(TO_X, 1 - t, e)
     send(TO_CORE, 1 - t, e)
@@ -281,7 +282,7 @@
                 line, valid = at(distance - 1, sign)
                 owner = owner_at(line, 1 - b)
                 arrive(t, owner, valid)
-                send(TO_Y, t, owner, valid)
+                send(TO_Y, t, owner, valid & (line != pair))
                 send(TO_CORE, t, owner, valid)
     owner = owner_at(a, 1 - b)
     arrive(1 - t, owner)
@@ -289,17 +290,38 @@
     for distance in range(1, LINES):
         for sign in (-1, 1):
             line, valid = at(distance, sign)
-            for x in (b, 1 - b):
-                owner = owner_at(line, x)
-                arrive(1 - t, owner, valid)
-                send(TO_CORE, 1 - t, owner, valid)
+            owner = owner_at(line, b)
+            arrive(1 - t, owner, valid)
+            if distance == 1:
+                send(TO_X, 1 - t, owner, valid & (line == pair))
+            send(TO_CORE, 1 - t, owner, valid)
     for line in range(LINES):
         for x in range(2):
-            for h in range(2):
-                arrive(h, line * 4 + x * 2 + 1 - c)
+            arrive(t, line * 4 + x * 2 + 1 - c)
+
+    def half_product(matrix, h, first, count):
+        depth = pl.ds(pl.multiple_of(h * half, half), half)
+        tokens = rows[h, pl.ds(first, count), :, :half].reshape(count * group, half)
+        return jnp.dot(tokens, matrix[depth, :], preferred_element_type=jnp.float32)
+
+    def far_x(distance):
+        for sign in (-1, 1):
+            line, valid = at(distance, sign)
+            owner = owner_at(line, 1 - b)
+            arrive(1 - t, owner, valid)
+            send(TO_CORE, 1 - t, owner, valid)
 
     loads[4].wait()
+    gate_acc[...] = half_product(gate, t, 0, experts)
+    far_x(1)
     loads[5].wait()
+    up_acc[...] = half_product(up, t, 0, experts)
+    far_x(2)
+    far_x(3)
+    for line in range(LINES):
+        for x in range(2):
+            arrive(1 - t, line * 4 + x * 2 + 1 - c)
+
     near = a // 2
     parts = (1 - near, near)
     side = lax.rem(a, 2)
@@ -339,15 +361,9 @@
         )
 
     def front(p):
-        left = rows[0, pl.ds(parts[p] * 8, 8), :, :half].reshape(part_rows, half)
-        right = rows[1, pl.ds(parts[p] * 8, 8), :, :half].reshape(part_rows, half)
-
-        def act(matrix):
-            return jnp.dot(left, matrix[:half, :], preferred_element_type=jnp.float32) + jnp.dot(
-                right, matrix[half:, :], preferred_element_type=jnp.float32
-            )
-
-        gate_act, up_act = act(gate), act(up)
+        span = pl.ds(pl.multiple_of(parts[p] * part_rows, part_rows), part_rows)
+        gate_act = gate_acc[span, :] + half_product(gate, 1 - t, parts[p] * 8, 8)
+        up_act = up_acc[span, :] + half_product(up, 1 - t, parts[p] * 8, 8)
         hidden = (gate_act / (1.0 + jnp.exp(-gate_act)) * up_act).astype(jnp.bfloat16)
         first = lax.rem(lines[2 * p], 2)
         hid_own[2 * p + first] = hidden[:line_rows]
@@ -456,6 +472,8 @@
             pltpu.VMEM(gate_proj.shape[1:], bf),
             pltpu.VMEM(up_proj.shape[1:], bf),
             pltpu.VMEM(down_proj.shape[1:], bf),
+            pltpu.VMEM((LINES * line_rows, units), f32),
+            pltpu.VMEM((LINES * line_rows, units), f32),
             pltpu.VMEM((LINES, line_rows, units), bf),
             pltpu.VMEM((LINES, line_rows, units), bf),
             pltpu.VMEM((LINES, 4, group, half), f32),

time: 49.3 us -> 50.4 us (1.022)
  Pallas kernels: 47.6 us -> 48.8 us
    pallas_call x1, Pallas kernels: 47.6 us -> 48.8 us  [dense_on_device(): pl.pallas_call(dense_kernel, out_shape=jax.ShapeDtypeStruct((group // 2,...]
where the time goes in v3:
time: 50.4 us; the launch traced here: 50.2 us
  Pallas kernels  48.8 us (97%)
  local copies, waits for them, and re-layouts  1.47 us (3%)
    pallas_call x1, Pallas kernels, dense_on_device(): pl.pallas_call(dense_kernel, out_shape=jax.ShapeDtypeStruct((group // 2,...  48.8 us
    unnamed x1, local copies, waits for them, and re-layouts  1.47 us

profile of v3, /device:TPU:0, one launch (start us, length us, event | category | flops | bytes accessed | tf_op | source)
XLA Modules:
  0.0 50.2 jit_solution(4860690363446302333)
XLA Ops:
  0.0 48.8 %shard_map.73 = bf16[8,4096]{1,0:T(8,128)(2,1)} custom-call(bf16[16,4096]{1,0:T(8,128)(2,1)} %bitcast.10, f32[1,4096]{1,0:T(1,128)} %bitcast.11, s32[8,16]{1,0:T(8,128)} %bitcast.12, f32[8,16]{1,0:T(8,128)} %bitcast.13, bf16[4096,512]{1,0:T(8,128)(2,1)} %bitcast.7, bf16[4096,512]{1,0:T(8,128)(2,1)} %bitcast.8, bf16[1024,2048]{1,0:T(8,128)(2,1)} %bitcast.9), custom_call_target="tpu_custom_call" | custom-call | tf_op jit(solution)/shard_map/pallas_call | solution.py:459
  48.8 1.5 %copy.9 = bf16[8,4096]{1,0:T(8,128)(2,1)} copy(bf16[8,4096]{1,0:T(8,128)(2,1)} %shard_map.73) | data formatting | bytes 131072

commit v4 on v3

--- a/solution.py
+++ b/solution.py
@@ -142,14 +142,14 @@
 
 LINES = 4
 MESH = pl.DeviceIdType.MESH
-TO_Y, TO_X, TO_CORE = range(3)
+TO_Y, TO_X, TO_CORE, TO_UP, TO_DOWN = range(5)
 
 
 def dense_kernel(
     attn_hbm, gain_hbm, ids_hbm, weights_hbm, gate_hbm, up_hbm, down_hbm, out,
     attn, gain, ids, weights, table, rows, other, gate, up, down, gate_acc, up_acc, hid_own, hid_in, total, core_out, core_in,
     x_out, x_in, z_out, z_in, swap_out, swap_in,
-    load_sem, attn_sem, row_send, line_send, row_recv, hid_sem, core_sem, x_sem, z_send, z_recv, swap_sem,
+    load_sem, attn_sem, row_send, row_recv, hid_sem, core_sem, x_sem, z_send, z_recv, swap_sem,
 ):
     t = lax.axis_index("tensor")
     e = lax.axis_index("expert")
@@ -161,6 +161,8 @@
         TO_Y: {"tensor": 1 - t, "expert": e},
         TO_X: {"tensor": t, "expert": e + 2 - 4 * b},
         TO_CORE: {"tensor": t, "expert": e + 1 - 2 * c},
+        TO_UP: {"tensor": t, "expert": e + 4},
+        TO_DOWN: {"tensor": t, "expert": e - 4},
     }
 
     loads = [
@@ -243,32 +245,21 @@
         valid = (line >= 0) & (line < LINES)
         return jnp.clip(line, 0, LINES - 1), valid
 
-    def line_piece(h, line):
-        return pltpu.make_async_remote_copy(
-            src_ref=rows.at[h, e], dst_ref=rows.at[h, e], send_sem=line_send.at[h, line],
-            recv_sem=row_recv.at[h, e], device_id={"tensor": t, "expert": owner_at(line, b)},
-            device_id_type=MESH,
-        )
-
-    def along_line(act):
-        for h, distances in ((t, range(1, LINES)), (1 - t, (1,))):
-            for distance in distances:
-                for sign in (-1, 1):
-                    line, valid = at(distance, sign)
-                    pl.when(valid)(functools.partial(act, h, line))
-
+    upper, lower = a < LINES - 1, a > 0
+    send(TO_UP, t, e, upper)
+    send(TO_DOWN, t, e, lower)
     send(TO_X, t, e)
     send(TO_CORE, t, e)
-    pair = a + 1 - 2 * lax.rem(a, 2)
-    along_line(lambda h, line: line_piece(h, line).start())
-    send(TO_X, 1 - t, e)
-    send(TO_CORE, 1 - t, e)
-    for distance in range(1, LINES + 2):
+    for distance in range(1, LINES + 1):
         if distance < LINES:
             for sign in (-1, 1):
                 line, valid = at(distance, sign)
                 owner = owner_at(line, b)
                 arrive(t, owner, valid)
+                if sign < 0:
+                    send(TO_UP, t, owner, valid & upper)
+                else:
+                    send(TO_DOWN, t, owner, valid & lower)
                 send(TO_X, t, owner, valid)
                 if distance >= 2:
                     send(TO_Y, t, owner, valid)
@@ -277,13 +268,18 @@
             owner = owner_at(a, 1 - b)
             arrive(t, owner)
             send(TO_CORE, t, owner)
-        elif distance <= LINES:
+            send(TO_UP, 1 - t, e, upper)
+            send(TO_DOWN, 1 - t, e, lower)
+            send(TO_CORE, 1 - t, e)
+        else:
             for sign in (-1, 1):
                 line, valid = at(distance - 1, sign)
                 owner = owner_at(line, 1 - b)
                 arrive(t, owner, valid)
-                send(TO_Y, t, owner, valid & (line != pair))
+                send(TO_Y, t, owner, valid)
                 send(TO_CORE, t, owner, valid)
+        if distance == 2:
+            send(TO_X, 1 - t, e)
     owner = owner_at(a, 1 - b)
     arrive(1 - t, owner)
     send(TO_CORE, 1 - t, owner)
@@ -292,12 +288,7 @@
             line, valid = at(distance, sign)
             owner = owner_at(line, b)
             arrive(1 - t, owner, valid)
-            if distance == 1:
-                send(TO_X, 1 - t, owner, valid & (line == pair))
             send(TO_CORE, 1 - t, owner, valid)
-    for line in range(LINES):
-        for x in range(2):
-            arrive(t, line * 4 + x * 2 + 1 - c)
 
     def half_product(matrix, h, first, count):
         depth = pl.ds(pl.multiple_of(h * half, half), half)
@@ -311,12 +302,15 @@
             arrive(1 - t, owner, valid)
             send(TO_CORE, 1 - t, owner, valid)
 
+    far_x(1)
+    for line in range(LINES):
+        for x in range(2):
+            arrive(t, line * 4 + x * 2 + 1 - c)
     loads[4].wait()
     gate_acc[...] = half_product(gate, t, 0, experts)
-    far_x(1)
+    far_x(2)
     loads[5].wait()
     up_acc[...] = half_product(up, t, 0, experts)
-    far_x(2)
     far_x(3)
     for line in range(LINES):
         for x in range(2):
@@ -368,11 +362,12 @@
         first = lax.rem(lines[2 * p], 2)
         hid_own[2 * p + first] = hidden[:line_rows]
         hid_own[2 * p + 1 - first] = hidden[line_rows:]
-        for q in (2 * p, 2 * p + 1):
-            hidden_copy(q).start()
+        hidden_copy(p).start()
 
     def back(q):
         hidden_copy(q).wait_recv()
+        if q < 2:
+            hidden_copy(q + 2).start()
         mine = pl.ds(pl.multiple_of(t * units, units), units)
         theirs = pl.ds(pl.multiple_of((1 - t) * units, units), units)
         acc = jnp.dot(hid_own[q], down[mine, :], preferred_element_type=jnp.float32)
@@ -435,7 +430,6 @@
             piece(kind, h, owner).wait_send()
         else:
             pl.when(when)(functools.partial(lambda k, i, o: piece(k, i, o).wait_send(), kind, h, owner))
-    along_line(lambda h, line: line_piece(h, line).wait_send())
     for p in range(LINES):
         hidden_copy(p).wait_send()
         core_copy(p).wait_send()
@@ -485,7 +479,7 @@
             pltpu.VMEM((LINES, group, half), bf),
             pltpu.VMEM((group, half // 2), bf),
             pltpu.VMEM((group, half // 2), bf),
-            dma((7,)), dma((2,)), dma((3, 2, experts)), dma((2, LINES)), dma((2, experts)),
+            dma((7,)), dma((2,)), dma((5, 2, experts)), dma((2, experts)),
             dma((2, LINES)), dma((2, LINES)), dma((2, LINES)), dma((LINES,)), dma((LINES,)), dma((2,)),
         ],
         compiler_params=pltpu.CompilerParams(

time: 50.4 us -> 50.8 us (level)
  no operation moved by 1% of the time
where the time goes in v4:
time: 50.8 us; the launch traced here: 50.6 us
  Pallas kernels  49.1 us (97%)
  local copies, waits for them, and re-layouts  1.47 us (3%)
    pallas_call x1, Pallas kernels, dense_on_device(): pl.pallas_call(dense_kernel, out_shape=jax.ShapeDtypeStruct((group // 2,...  49.1 us
    unnamed x1, local copies, waits for them, and re-layouts  1.47 us

profile of v4, /device:TPU:0, one launch (start us, length us, event | category | flops | bytes accessed | tf_op | source)
XLA Modules:
  0.0 50.6 jit_solution(12956619823702457515)
XLA Ops:
  0.0 49.1 %shard_map.73 = bf16[8,4096]{1,0:T(8,128)(2,1)} custom-call(bf16[16,4096]{1,0:T(8,128)(2,1)} %bitcast.10, f32[1,4096]{1,0:T(1,128)} %bitcast.11, s32[8,16]{1,0:T(8,128)} %bitcast.12, f32[8,16]{1,0:T(8,128)} %bitcast.13, bf16[4096,512]{1,0:T(8,128)(2,1)} %bitcast.7, bf16[4096,512]{1,0:T(8,128)(2,1)} %bitcast.8, bf16[1024,2048]{1,0:T(8,128)(2,1)} %bitcast.9), custom_call_target="tpu_custom_call" | custom-call | tf_op jit(solution)/shard_map/pallas_call | solution.py:453
  49.1 1.5 %copy.9 = bf16[8,4096]{1,0:T(8,128)(2,1)} copy(bf16[8,4096]{1,0:T(8,128)(2,1)} %shard_map.73) | data formatting | bytes 131072
